TPU v7x, 1024 devices: a whole 4x8x16 slice. The times are simulated.
1024 devices in a mesh: pop: 16 (over y, z_hi), fsdp: 64 (over x, z_lo, core).
Axes of the slice: x: 4, y: 8, z: 16 (z_hi: 2, z_lo: 8; z = z_hi * 8 + z_lo), core: 2. Of those that a mesh axis runs over, the one named last changes fastest.
Arguments:
- weight: float32 [14336, 8192], P('fsdp', 'pop'), may hold values from -6 to 6
- first_moment: float32 [14336, 8192], P('fsdp', 'pop'), may hold values from -4 to 4
- second_moment: float32 [14336, 8192], P('fsdp', 'pop'), may hold values from 0.0001 to 0.01
- row_factors: bfloat16 [1024, 4, 14336], P('pop', None, 'fsdp'), may hold values from -6 to 6
- column_factors: bfloat16 [1024, 4, 8192], P(None, None, ('pop', 'fsdp')), may hold values from -6 to 6
- scores: int32 [1024], P('pop'), may hold values from 0 to 799, as said below
Outputs:
- new_weight: float32 [14336, 8192], P('fsdp', 'pop')
- new_first: float32 [14336, 8192], P('fsdp', 'pop')
- new_second: float32 [14336, 8192], P('fsdp', 'pop')
Inputs may be any that keep to these rules, and one draw needn't show every extreme that they name: Integer fitness scores; the lowest and the highest possible score both occur.
All inputs are finite; a program needn't handle non-finite values.
Results may differ from a plain program's by a relative error of at most 0.0017.
Values may be sent and summed in bfloat16 or wider, within the bound.
A program may use at most 32 MiB of HBM per device.

v0:
```python
import math

import jax
import jax.numpy as jnp
from jax import lax
from jax.sharding import PartitionSpec as P

ADAM_STEP = 10


beta_one = 0.9
beta_two = 0.999
learn_rate = 0.05
adam_eps = 1e-08
score_eps = 1e-05


def fitness_from(score_total, squares, values, members):
    average = score_total / members
    variance = squares / members - average * average
    return (values - average) * lax.rsqrt(variance + score_eps)


def local(weight, first_moment, second_moment, row_factors, column_factors, scores):
    members_dev = row_factors.shape[0]
    factor_rank = row_factors.shape[1]
    row_count = row_factors.shape[2]
    members = members_dev * lax.axis_size("pop")
    values = scores.astype(jnp.float32)
    score_total, squares = lax.psum((jnp.sum(values), jnp.sum(values * values)), "pop")
    fitness = fitness_from(score_total, squares, values, members)
    local_weighted = (fitness[:, None, None] * row_factors.astype(jnp.float32)).astype(jnp.bfloat16)
    columns = lax.all_gather(column_factors, "fsdp", axis=2, tiled=True)
    col_width = columns.shape[2]
    left_rows = lax.all_gather(local_weighted, "pop", axis=0, tiled=True)
    count = left_rows.shape[0]
    update = lax.dot_general(
        left_rows.reshape(count * factor_rank, row_count),
        columns.reshape(count * factor_rank, col_width),
        (((0,), (0,)), ((), ())),
        preferred_element_type=jnp.float32,
    )
    update = update / math.sqrt(members * factor_rank)
    new_first = beta_one * first_moment + (1.0 - beta_one) * update
    new_second = beta_two * second_moment + (1.0 - beta_two) * update * update
    corrected_first = new_first / (1.0 - beta_one**ADAM_STEP)
    corrected_second = new_second / (1.0 - beta_two**ADAM_STEP)
    new_weight = weight + learn_rate * corrected_first / (jnp.sqrt(corrected_second) + adam_eps)
    return (new_weight, new_first, new_second)


def solution(mesh):
    in_specs = (
        P("fsdp", "pop"),
        P("fsdp", "pop"),
        P("fsdp", "pop"),
        P("pop", None, "fsdp"),
        P(None, None, ("pop", "fsdp")),
        P("pop"),
    )
    out_specs = (P("fsdp", "pop"), P("fsdp", "pop"), P("fsdp", "pop"))
    return jax.shard_map(local, mesh=mesh, in_specs=in_specs, out_specs=out_specs, check_vma=False)
```

profile of v0, /device:TPU:1, one launch (start us, length us, event | category | flops | bytes accessed | tf_op | source)
XLA Modules:
  0.0 373.7 jit_solution(13057679394406839531)
XLA Ops:
  7.2 0.0 all-gather.3.cloned.1.call-start
  7.2 1.3 convert_reduce_fusion
  8.5 80.5 %all-reduce = (f32[]{:T(128)}, f32[]{:T(128)}) all-reduce(f32[]{:T(128)} %get-tuple-element.4, f32[]{:T(128)} %get-tuple-element.3), channel_id=1, replica_groups=mesh['pop'=16,'fsdp'=64] {'pop'}, use_global_device_ids=true, to_apply=%region_3.0 | all-reduce | flops 2 | bytes 16 | tf_op jit(solution)/shard_map/psum | solution.py:30
  91.6 0.7 subtract_multiply_fusion
  92.2 1.6 multiply_convert_fusion
  93.9 0.0 all-gather.3.cloned.1.call-update
  93.9 0.0 all-gather.5.cloned.1.call-start
  94.0 0.7 all-gather.5.cloned.1.call-update
  94.7 144.5 %all-gather.3.cloned.1.call-done = bf16[1024,4,224]{2,0,1:T(8,128)(2,1)} async-done(((bf16[64,4,224]{2,0,1:T(8,128)(2,1)}), bf16[1024,4,224]{2,0,1:T(8,128)(2,1)}) %all-gather.3.cloned.1.call-update) | async-done | bytes 1835024 | tf_op jit(solution)/shard_map/all_gather | solution.py:35
  239.2 121.8 %all-gather.5.cloned.1.call-done = bf16[1024,4,512]{0,2,1:T(8,128)(2,1)} async-done(((bf16[1024,4,8]{0,2,1:T(8,128)(2,1)}), bf16[1024,4,512]{0,2,1:T(8,128)(2,1)}) %all-gather.5.cloned.1.call-update) | async-done | bytes 4194320 | tf_op jit(solution)/shard_map/all_gather | solution.py:33
  361.0 5.9 %divide_add_fusion = (f32[224,512]{1,0:T(8,128)}, f32[224,512]{1,0:T(8,128)}, f32[224,512]{1,0:T(8,128)}) fusion(f32[224,512]{1,0:T(8,128)} %param.6, f32[224,512]{1,0:T(8,128)} %param.7, f32[224,512]{1,0:T(8,128)} %param.8, bf16[1024,4,224]{2,0,1:T(8,128)(2,1)} %all-gather.3.cloned.1.call-done, bf16[1024,4,512]{0,2,1:T(8,128)(2,1)} %all-gather.5.cloned.1.call-done), kind=kOutput, calls=%fused_computation.1 | convolution fusion | flops 941015040 | bytes 8781824 | tf_op jit(solution)/shard_map/dot_general | solution.py:37
Async XLA Ops:
  7.2 232.0 %all-gather.3.cloned.1.call-start = ((), (), s32[]{:S(2)}) async-start(), calls=%async_computation | async-start | bytes 2228224 | tf_op jit(solution)/shard_map/all_gather | solution.py:35
  93.9 267.1 %all-gather.5.cloned.1.call-start = ((), (), s32[]{:S(2)}) async-start(), calls=%async_computation.1 | async-start | bytes 4259840 | tf_op jit(solution)/shard_map/all_gather | solution.py:33
Sparse Core Ops, SparseCore 0:
  94.0 145.1 all-gather.2
  241.9 118.9 all-gather.4
where the time goes:
time: 374 us
  waiting for transfers between devices  267 us (71%)
  blocking collectives  80.5 us (22%)
  between operations  16.7 us (4%)
  matrix products  5.91 us (2%)
    all_gather x1, waiting for transfers between devices, local(): left_rows = lax.all_gather(local_weighted, 'pop', axis=0, tiled=True)  145 us
    all_gather x1, waiting for transfers between devices, local(): columns = lax.all_gather(column_factors, 'fsdp', axis=2, tiled=True)  122 us
    psum x1, blocking collectives, local(): lax.psum((jnp.sum(values), jnp.sum(values * values)), 'pop')  80.5 us
  transfers between devices with their start and end apart: 2, of which 2 were waited for; matrix products, arithmetic and copies ran while one was open for 0% of the time, Pallas kernels for 0%

commit v1 on v0

v1 whole, which is shorter than its diff:
```python
import functools
import math

import jax
import jax.numpy as jnp
from jax import lax
from jax.experimental import pallas as pl
from jax.experimental.pallas import tpu as pltpu
from jax.sharding import PartitionSpec as P

ADAM_STEP = 10
MESH = pl.DeviceIdType.MESH

beta_one = 0.9
beta_two = 0.999
learn_rate = 0.05
adam_eps = 1e-08
score_eps = 1e-05

NX, NY, NZ, RUN = 4, 8, 16, 8
POP = 16
ROWS = 224
COLS = 512
KEEP = 2048
SLOT = 2 * ROWS + 16
T_Y, T_Z4, T_C, T_C4, T_X, T_SIB = 3.3, 5.5, 3.0, 4.5, 3.0, 1.5


def device_at(x, y, z, c):
    x, y, z = (x + NX) % NX, (y + NY) % NY, (z + NZ) % NZ
    return (y * 2 + z // RUN, (x * RUN + z % RUN) * 2 + c)


def swap_lanes(even, odd):
    low = lax.broadcasted_iota(jnp.int32, (even.shape[0], 128), 1) < 64
    parts = []
    for t in range(8):
        a = even[:, t * 128 : (t + 1) * 128]
        b = odd[:, t * 128 : (t + 1) * 128]
        parts.append(jnp.where(low, a, pltpu.roll(b, 64, 1)))
        parts.append(jnp.where(low, pltpu.roll(a, 64, 1), b))
    return jnp.concatenate(parts, axis=1)


def kernel(
    row_ref, col_ref, score_ref, out_ref,
    rowbuf, transit, colbuf, row_out, col_out, col_in, wbuf, part_out, part_in,
    sem_sib_s, sem_sib_r, sem_z4_s, sem_z4_r, sem_y_s, sem_y_r,
    sem_c_s, sem_c_r, sem_x_s, sem_x_r, sem_f_s, sem_f_r,
):
    p = lax.axis_index("pop")
    f = lax.axis_index("fsdp")
    y, zh = p // 2, p % 2
    c, zl, x = f % 2, (f // 2) % RUN, f // (2 * RUN)
    z = zh * RUN + zl
    turn = 1 - 2 * c

    partners = [
        device_at(x, y, z, 1 - c),
        device_at(x, y + 1, z, c), device_at(x, y + NY - 1, z, c),
        device_at(x + 1, y, z, c), device_at(x + NX - 1, y, z, c),
        device_at(x, y, z + 1, c), device_at(x, y, z + NZ - 1, c),
        device_at(x, y, z + 4, c), device_at(x, y, z + NZ - 4, c),
    ]
    sibling = partners[0]
    barrier = pltpu.get_barrier_semaphore()
    for dev in partners:
        pl.semaphore_signal(barrier, inc=1, device_id=dev, device_id_type=MESH)

    rows = jnp.swapaxes(row_ref[...], 0, 1)
    halves = [rows[2 * q : 2 * q + 2].reshape(128, ROWS).T for q in range(2)]
    mine = jnp.where(c == 0, halves[0], halves[1])
    theirs = jnp.where(c == 0, halves[1], halves[0])
    own_rows = pl.multiple_of(c * (ROWS + 16), 16)
    rowbuf[p, pl.ds(own_rows, ROWS), :] = mine
    row_out[...] = theirs
    score = score_ref[...]
    score = jnp.concatenate([score, score], axis=1)
    line = lax.broadcasted_iota(jnp.int32, (16, 128), 0)
    coded = jnp.where(line == 0, score // 16, jnp.where(line == 1, score % 16, 0))
    rowbuf[p, ROWS : ROWS + 16, :] = coded.astype(jnp.float32).astype(jnp.bfloat16)
    blocks = [col_ref[k].astype(jnp.float32) for k in range(4)]
    wide = [swap_lanes(blocks[2 * q], blocks[2 * q + 1]) for q in range(2)]
    my_cols = jnp.where(c == 0, wide[0], wide[1])
    col_out[...] = jnp.where(c == 0, wide[1], wide[0]).astype(jnp.bfloat16)

    pl.semaphore_wait(barrier, len(partners))

    sends = []

    def remote(src, dst, s_sem, r_sem, dev):
        return pltpu.make_async_remote_copy(
            src_ref=src, dst_ref=dst, send_sem=s_sem, recv_sem=r_sem, device_id=dev, device_id_type=MESH
        )

    def go(copy, when=None):
        if when is None:
            copy.start()
        else:
            pl.when(when)(copy.start)
        sends.append((when, copy))

    first_len = ROWS + 16

    def piece(buf, slot, n):
        if n == 0:
            start, length = c * ROWS, first_len
        else:
            start, length = (1 - c) * first_len, ROWS
        start = pl.multiple_of(start, 16)
        return buf.at[pl.ds(start, length)] if slot is None else buf.at[slot, pl.ds(start, length)]

    def y_copy(stream, way, hop, n):
        d = turn if way == 0 else -turn
        src_y = (y - d * (hop - 1) + 2 * NY) % NY
        slot = src_y * 2 + (zh if stream == 0 else 1 - zh)
        ref = piece(rowbuf, slot, n)
        i = stream * 2 + way
        return remote(ref, ref, sem_y_s.at[i, hop - 1, n], sem_y_r.at[i, hop - 1, n], device_at(x, y + d, z, c))

    def y_wait(stream, way, hop, n):
        y_copy(stream, way, hop, n).wait_recv()

    far = device_at(x, y, z + 4 * turn + NZ, c)
    behind = (z - 4 * turn + NZ) % NZ

    def z4_copy(stage, n):
        if stage == 0:
            src, dst = piece(rowbuf, p, n), piece(transit, None, n)
        else:
            src, dst = piece(transit, None, n), piece(rowbuf, y * 2 + behind // RUN, n)
        return remote(src, dst, sem_z4_s.at[stage, n], sem_z4_r.at[stage, n], far)

    def col_block(x_at, zl_at, half=None):
        at = pl.ds(pl.multiple_of((x_at * RUN + zl_at) * 16, 16), 16)
        if half is None:
            return colbuf.at[at]
        return colbuf.at[at, pl.ds(half * (KEEP // 2), KEEP // 2)]

    def c_copy(way, d):
        step = 1 - 2 * way
        origin = zl - step * (0 if d == 4 else d - 1)
        ref = col_block(x, origin)
        jump = 4 if d == 4 else 1
        return remote(ref, ref, sem_c_s.at[way, d - 1], sem_c_r.at[way, d - 1], device_at(x, y, z + step * jump + NZ, c))

    def inside(v):
        return jnp.logical_and(v >= 0, v < RUN)

    def c_send(way, d):
        step = 1 - 2 * way
        origin = zl - step * (0 if d == 4 else d - 1)
        target = zl + step * (4 if d == 4 else 1)
        go(c_copy(way, d), jnp.logical_and(inside(origin), inside(target)))

    def c_origin(way, d):
        return zl - (1 - 2 * way) * d

    def x_send(zl_at, when):
        for way in range(2):
            step = 1 - 2 * way
            ref = col_block(x, zl_at)
            at = jnp.clip(zl_at, 0, RUN - 1)
            go(remote(ref, ref, sem_x_s.at[way, at], sem_x_r.at[way, at], device_at(x + step + NX, y, z, c)), when)

    def x_pass(zl_at, when):
        for way in range(2):
            step = 1 - 2 * way
            at = jnp.clip(zl_at, 0, RUN - 1)
            x_at = (x - step + NX) % NX
            ref = col_block(x_at, zl_at)
            got = remote(ref, ref, sem_x_s.at[way, at], sem_x_r.at[way, at], device_at(x + step + NX, y, z, c))
            half = col_block(x_at, zl_at, way)
            on = remote(half, half, sem_f_s.at[way, at], sem_f_r.at[way, at], device_at(x + step + NX, y, z, c))
            if when is None:
                got.wait_recv()
            else:
                pl.when(when)(got.wait_recv)
            go(on, when)

    events = []

    def at_time(t, fn):
        events.append((t, len(events), fn))

    sib_rows = remote(row_out, rowbuf.at[p, pl.ds(own_rows, ROWS)], sem_sib_s.at[0], sem_sib_r.at[0], sibling)
    sib_cols = remote(col_out, col_in, sem_sib_s.at[1], sem_sib_r.at[1], sibling)

    def start():
        go(sib_cols)
        go(sib_rows)
        go(z4_copy(0, 0))
        go(y_copy(0, 0, 1, 0))
        go(y_copy(0, 1, 1, 0))

    def columns():
        sib_cols.wait_recv()
        other = col_in[...].astype(jnp.float32)
        both = jnp.concatenate([jnp.where(c == 0, my_cols, other), jnp.where(c == 0, other, my_cols)], axis=0)
        col_block(x, zl)[...] = both.astype(jnp.bfloat16)
        for d in (1, 4):
            for way in range(2):
                c_send(way, d)
        x_send(zl, None)

    def rows_second():
        sib_rows.wait_recv()
        go(z4_copy(0, 1))
        go(y_copy(0, 0, 1, 1))
        go(y_copy(0, 1, 1, 1))

    at_time(0.0, start)
    at_time(T_SIB, columns)
    at_time(T_SIB + 0.3, rows_second)

    def y_event(stream, way, hop, n):
        y_wait(stream, way, hop, n)
        if hop < (4 if way == 0 else 3):
            go(y_copy(stream, way, hop + 1, n))

    def z4_event(stage, n):
        z4_copy(stage, n).wait_recv()
        if stage == 0:
            go(z4_copy(1, n))
        else:
            go(y_copy(1, 0, 1, n))
            go(y_copy(1, 1, 1, n))

    for n in range(2):
        t0 = 0.0 if n == 0 else T_SIB + 0.3
        for stage in range(2):
            at_time(t0 + T_Z4 * (stage + 1), functools.partial(z4_event, stage, n))
        for stream in range(2):
            base = t0 + (0.0 if stream == 0 else 2 * T_Z4)
            for hop in range(1, 5):
                for way in range(2):
                    if hop <= (4 if way == 0 else 3):
                        at_time(base + T_Y * hop, functools.partial(y_event, stream, way, hop, n))

    def c_event(way, d):
        origin = c_origin(way, d)
        valid = inside(origin)
        step = 1 - 2 * way
        ref = col_block(x, origin)
        got = remote(
            ref, ref, sem_c_s.at[way, d - 1], sem_c_r.at[way, d - 1], device_at(x, y, z + step + NZ, c)
        )
        pl.when(valid)(got.wait_recv)
        if d not in (3, 7):
            c_send(way, d + 1)
        x_send(origin, valid)

    def x_event(way, d):
        origin = c_origin(way, d)
        x_pass(origin, inside(origin))

    at_time(T_SIB + T_X, lambda: x_pass(zl, None))
    for d in range(1, 8):
        for way in range(2):
            t = T_SIB + (T_C * d if d < 4 else T_C4 + T_C * (d - 4))
            at_time(t, functools.partial(c_event, way, d))
            at_time(t + T_X, functools.partial(x_event, way, d))

    for _, _, fn in sorted(events, key=lambda e: e[:2]):
        fn()

    for way in range(2):
        step = 1 - 2 * way
        for zl_at in range(RUN):
            half = col_block((x + 2) % NX, zl_at, way)
            remote(
                half, half, sem_f_s.at[way, zl_at], sem_f_r.at[way, zl_at], device_at(x + step + NX, y, z, c)
            ).wait_recv()

    tags = [rowbuf[i, ROWS : ROWS + 16, :].astype(jnp.float32) for i in range(POP)]
    values = [t[0:1] * 16.0 + t[1:2] for t in tags]
    values = jnp.concatenate(values, axis=0)
    members = POP * 64
    average = jnp.sum(values) * 0.5 / members
    variance = jnp.sum(values * values) * 0.5 / members - average * average
    fitness = (values - average) * lax.rsqrt(variance + score_eps)

    for i in range(POP):
        for h in range(2):
            block = rowbuf[i, h * first_len : h * first_len + ROWS, :].astype(jnp.float32)
            wbuf[h, :, i * 128 : (i + 1) * 128] = (block * fitness[i : i + 1]).astype(jnp.bfloat16)

    def product(h):
        return lax.dot_general(
            wbuf[h], colbuf[...], (((1,), (1,)), ((), ())), preferred_element_type=jnp.float32
        )

    part_out[...] = product(1 - c)
    swap = remote(part_out, part_in, sem_sib_s.at[2], sem_sib_r.at[2], sibling)
    swap.start()
    own = product(c)
    for when, copy in sends:
        if when is None:
            copy.wait_send()
        else:
            pl.when(when)(copy.wait_send)
    swap.wait()
    out_ref[...] = (own + part_in[...]) * (1.0 / 64.0)


def local(weight, first_moment, second_moment, row_factors, column_factors, scores):
    columns = jnp.transpose(column_factors, (1, 2, 0))
    dma = pltpu.SemaphoreType.DMA
    update = pl.pallas_call(
        kernel,
        name="gather_update",
        out_shape=jax.ShapeDtypeStruct((ROWS, COLS), jnp.float32),
        in_specs=[pl.BlockSpec(memory_space=pltpu.VMEM)] * 3,
        out_specs=pl.BlockSpec(memory_space=pltpu.VMEM),
        scratch_shapes=[
            pltpu.VMEM((POP, SLOT, 128), jnp.bfloat16),
            pltpu.VMEM((SLOT, 128), jnp.bfloat16),
            pltpu.VMEM((COLS, KEEP), jnp.bfloat16),
            pltpu.VMEM((ROWS, 128), jnp.bfloat16),
            pltpu.VMEM((8, KEEP), jnp.bfloat16),
            pltpu.VMEM((8, KEEP), jnp.bfloat16),
            pltpu.VMEM((2, ROWS, KEEP), jnp.bfloat16),
            pltpu.VMEM((ROWS, COLS), jnp.float32),
            pltpu.VMEM((ROWS, COLS), jnp.float32),
            dma((3,)), dma((3,)),
            dma((2, 2)), dma((2, 2)),
            dma((4, 4, 2)), dma((4, 4, 2)),
            dma((2, 7)), dma((2, 7)),
            dma((2, RUN)), dma((2, RUN)),
            dma((2, RUN)), dma((2, RUN)),
        ],
        compiler_params=pltpu.CompilerParams(
            collective_id=0, has_side_effects=True, vmem_limit_bytes=40 * 2**20
        ),
        cost_estimate=pl.CostEstimate(flops=2 * ROWS * COLS * 4096, bytes_accessed=2**20, transcendentals=0),
    )(row_factors, columns, scores.reshape(1, 64))
    new_first = beta_one * first_moment + (1.0 - beta_one) * update
    new_second = beta_two * second_moment + (1.0 - beta_two) * update * update
    corrected_first = new_first / (1.0 - beta_one**ADAM_STEP)
    corrected_second = new_second / (1.0 - beta_two**ADAM_STEP)
    new_weight = weight + learn_rate * corrected_first / (jnp.sqrt(corrected_second) + adam_eps)
    return (new_weight, new_first, new_second)


def solution(mesh):
    in_specs = (
        P("fsdp", "pop"),
        P("fsdp", "pop"),
        P("fsdp", "pop"),
        P("pop", None, "fsdp"),
        P(None, None, ("pop", "fsdp")),
        P("pop"),
    )
    out_specs = (P("fsdp", "pop"), P("fsdp", "pop"), P("fsdp", "pop"))
    return jax.shard_map(local, mesh=mesh, in_specs=in_specs, out_specs=out_specs, check_vma=False)
```

time: 374 us -> 71.9 us (0.19)
  waiting for transfers between devices: 267 us -> 0 us
  blocking collectives: 80.5 us -> 0 us
  Pallas kernels: 0 us -> 67.3 us
  between operations: 16.7 us -> 0.68 us
  matrix products: 5.91 us -> 0 us
    all_gather x2 -> x0, waiting for transfers between devices: 266 us -> none  [the longest x1 145 us: local(): left_rows = lax.all_gather(local_weighted, 'pop', axis=0, tiled=True)]
    psum x1 -> x0, blocking collectives: 80.5 us -> none  [local(): lax.psum((jnp.sum(values), jnp.sum(values * values)), 'pop')]
    pallas_call x0 -> x1, Pallas kernels: none -> 67.3 us  [local(): pl.pallas_call(kernel, name='gather_update', out_shape=jax.ShapeDtypeStru...]
    dot_general x1 -> x0, matrix products: 5.91 us -> none  [local(): lax.dot_general(left_rows.reshape(count * factor_rank, row_count), column...]
  transfers between devices with their start and end apart: 2 -> 0, of which waited for: 2 -> 0; matrix products, arithmetic and copies ran while one was open for 0% -> 0% of each run, Pallas kernels for 0% -> 0%
where the time goes in v1:
time: 71.9 us; the launch traced here: 71.7 us
  Pallas kernels  67.3 us (94%)
  local copies, waits for them, and re-layouts  2.4 us (3%)
  other arithmetic  1.28 us (2%)
    pallas_call x1, Pallas kernels, local(): pl.pallas_call(kernel, name='gather_update', out_shape=jax.ShapeDtypeStru...  67.3 us
    unnamed x12, local copies, waits for them, and re-layouts  2.4 us

profile of v1, /device:TPU:1, one launch (start us, length us, event | category | flops | bytes accessed | tf_op | source)
XLA Modules:
  0.0 71.7 jit_solution(4829116611227367663)
XLA Ops:
  0.6 0.0 copy-start.2
  0.6 0.6 copy-done.2
  1.3 0.0 copy-start
  1.3 0.9 %copy-done = bf16[64,4,224]{2,1,0:T(4,128)(2,1)S(1)} copy-done((bf16[64,4,224]{2,1,0:T(4,128)(2,1)S(1)}, bf16[64,4,224]{2,1,0:T(4,128)(2,1)}, u32[]{:S(2)}) %copy-start) | copy-done | bytes 114712
  2.2 0.0 copy-start.1
  2.2 0.8 %copy-done.1 = bf16[1024,4,8]{0,2,1:T(8,128)(2,1)S(1)} copy-done((bf16[1024,4,8]{0,2,1:T(8,128)(2,1)S(1)}, bf16[1024,4,8]{0,2,1:T(8,128)(2,1)}, u32[]{:S(2)}) %copy-start.1) | copy-done | bytes 65560
  3.0 0.0 copy-start.3
  3.0 0.0 copy-start.4
  3.0 0.0 copy-start.5
  3.0 67.3 %gather_update.1 = f32[224,512]{1,0:T(8,128)S(1)} custom-call(bf16[64,4,224]{2,1,0:T(4,128)(2,1)S(1)} %copy-done, bf16[4,8,1024]{2,1,0:T(8,128)(2,1)S(1)} %bitcast.2, s32[1,64]{1,0:T(1,128)S(1)} %bitcast.3), custom_call_target="tpu_custom_call" | custom-call | flops 939524096 | bytes 1048576 | tf_op jit(solution)/shard_map/gather_update/pallas_call | solution.py:309
  70.3 0.0 copy-done.3
  70.4 0.0 copy-done.4
  70.4 0.0 copy-done.5
  70.4 1.3 %divide_add_fusion = (f32[224,512]{1,0:T(8,128)}, f32[224,512]{1,0:T(8,128)}, f32[224,512]{1,0:T(8,128)}) fusion(f32[224,512]{1,0:T(8,128)S(1)} %copy-done.3, f32[224,512]{1,0:T(8,128)S(1)} %gather_update.1, f32[224,512]{1,0:T(8,128)S(1)} %copy-done.4, f32[224,512]{1,0:T(8,128)S(1)} %copy-done.5), kind=kLoop, calls=%fused_computation.2 | loop fusion | flops 1376256 | bytes 3211264 | tf_op jit(solution)/shard_map/add | solution.py:341
Async XLA Ops:
  0.6 0.7 copy-start.2
  1.3 0.9 %copy-start = (bf16[64,4,224]{2,1,0:T(4,128)(2,1)S(1)}, bf16[64,4,224]{2,1,0:T(4,128)(2,1)}, u32[]{:S(2)}) copy-start(bf16[64,4,224]{2,1,0:T(4,128)(2,1)} %row_ref.1) | copy-start | bytes 344068
  2.2 0.8 %copy-start.1 = (bf16[1024,4,8]{0,2,1:T(8,128)(2,1)S(1)}, bf16[1024,4,8]{0,2,1:T(8,128)(2,1)}, u32[]{:S(2)}) copy-start(bf16[1024,4,8]{0,2,1:T(8,128)(2,1)} %param.10) | copy-start | bytes 196612
  3.0 67.3 %copy-start.3 = (f32[224,512]{1,0:T(8,128)S(1)}, f32[224,512]{1,0:T(8,128)}, u32[]{:S(2)}) copy-start(f32[224,512]{1,0:T(8,128)} %param.6) | copy-start | bytes 1376260
  3.0 67.3 %copy-start.4 = (f32[224,512]{1,0:T(8,128)S(1)}, f32[224,512]{1,0:T(8,128)}, u32[]{:S(2)}) copy-start(f32[224,512]{1,0:T(8,128)} %param.7) | copy-start | bytes 1376260
  3.0 67.3 %copy-start.5 = (f32[224,512]{1,0:T(8,128)S(1)}, f32[224,512]{1,0:T(8,128)}, u32[]{:S(2)}) copy-start(f32[224,512]{1,0:T(8,128)} %param.8) | copy-start | bytes 1376260

commit v2 on v0

v2 whole, which is shorter than its diff:
```python
import functools
import math

import jax
import jax.numpy as jnp
from jax import lax
from jax.experimental import pallas as pl
from jax.experimental.pallas import tpu as pltpu
from jax.sharding import PartitionSpec as P

ADAM_STEP = 10
MESH = pl.DeviceIdType.MESH

beta_one = 0.9
beta_two = 0.999
learn_rate = 0.05
adam_eps = 1e-08
score_eps = 1e-05

NX, NY, NZ, RUN = 4, 8, 16, 8
POP = 16
ROWS = 224
COLS = 512
KEEP = 2048
SLOT = 2 * ROWS + 16
T_Y, T_C, T_C4, T_X, T_SIB, T_P = 3.3, 3.0, 4.5, 3.0, 2.0, 13.0


def device_at(x, y, z, c):
    x, y, z = (x + NX) % NX, (y + NY) % NY, (z + NZ) % NZ
    return (y * 2 + z // RUN, (x * RUN + z % RUN) * 2 + c)


def swap_lanes(even, odd):
    low = lax.broadcasted_iota(jnp.int32, (even.shape[0], 128), 1) < 64
    parts = [[], []]
    for t in range(8):
        a = even[:, t * 128 : (t + 1) * 128]
        b = odd[:, t * 128 : (t + 1) * 128]
        parts[0].append(jnp.where(low, a, pltpu.roll(b, 64, 1)))
        parts[1].append(jnp.where(low, pltpu.roll(a, 64, 1), b))
    return jnp.concatenate(parts[0] + parts[1], axis=1)


def kernel(
    row_hbm, col_hbm, score_hbm, out_ref,
    row_ref, col_ref, score_ref, rowbuf, tags, colbuf, row_out, col_out, col_in, wbuf, acc, part_in,
    sem_in, sem_sib_s, sem_sib_r, sem_z8_s, sem_z8_r, sem_tag_s, sem_tag_r, sem_y_s, sem_y_r,
    sem_c_s, sem_c_r, sem_x_s, sem_x_r, sem_f_s, sem_f_r,
):
    p = lax.axis_index("pop")
    f = lax.axis_index("fsdp")
    y, zh = p // 2, p % 2
    c, zl, x = f % 2, (f // 2) % RUN, f // (2 * RUN)
    z = zh * RUN + zl
    turn = 1 - 2 * c
    upper, lower = zh == 1, zh == 0

    loads = [
        pltpu.make_async_copy(src, dst, sem_in.at[i])
        for i, (src, dst) in enumerate(((row_hbm, row_ref), (score_hbm, score_ref), (col_hbm, col_ref)))
    ]
    for load in loads:
        load.start()

    sibling = device_at(x, y, z, 1 - c)
    partner = device_at(x, y, z + 8, c)
    barrier = pltpu.get_barrier_semaphore()

    def greet(dev):
        pl.semaphore_signal(barrier, inc=1, device_id=dev, device_id_type=MESH)

    greet(sibling)
    for dev in (device_at(x, y + 1, z, c), device_at(x, y - 1, z, c), device_at(x + 1, y, z, c), device_at(x - 1, y, z, c)):
        greet(dev)
    pl.when(zl < 7)(lambda: greet(device_at(x, y, z + 1, c)))
    pl.when(zl < 4)(lambda: greet(device_at(x, y, z + 4, c)))
    pl.when(lower)(lambda: greet(partner))
    expected = 5 + jnp.where(zl > 0, 1, 0) + jnp.where(zl >= 4, 1, 0) + zh

    first_len = ROWS + 16
    own_rows = pl.multiple_of(c * first_len, 16)
    loads[0].wait()
    loads[1].wait()
    rows = jnp.swapaxes(row_ref[...], 0, 1)
    halves = [rows[2 * q : 2 * q + 2].reshape(128, ROWS).T for q in range(2)]
    rowbuf[p, pl.ds(own_rows, ROWS), :] = jnp.where(c == 0, halves[0], halves[1])
    row_out[...] = jnp.where(c == 0, halves[1], halves[0])
    score = score_ref[...]
    score = jnp.concatenate([score, score], axis=1)
    line = lax.broadcasted_iota(jnp.int32, (16, 128), 0)
    coded = jnp.where(line == 0, score // 16, jnp.where(line == 1, score % 16, 0))
    rowbuf[p, ROWS : ROWS + 16, :] = coded.astype(jnp.float32).astype(jnp.bfloat16)

    pl.semaphore_wait(barrier, expected)

    early, late = [], []

    def remote(src, dst, s_sem, r_sem, dev):
        return pltpu.make_async_remote_copy(
            src_ref=src, dst_ref=dst, send_sem=s_sem, recv_sem=r_sem, device_id=dev, device_id_type=MESH
        )

    def only(when, fn):
        if when is None:
            fn()
        else:
            pl.when(when)(fn)

    def go(copy, when=None, group=early):
        only(when, copy.start)
        group.append((when, copy))

    def piece(slot, stream, n):
        if n == 1:
            start, length = (1 - c) * first_len, ROWS
        elif stream == 0:
            start, length = c * ROWS, first_len
        else:
            start, length = c * first_len, ROWS
        return rowbuf.at[slot, pl.ds(pl.multiple_of(start, 16), length)]

    def y_copy(stream, way, hop, n):
        d = turn if way == 0 else -turn
        src_y = (y - d * (hop - 1) + 2 * NY) % NY
        ref = piece(src_y * 2 + (zh if stream == 0 else 1 - zh), stream, n)
        i = stream * 2 + way
        return remote(ref, ref, sem_y_s.at[i, hop - 1, n], sem_y_r.at[i, hop - 1, n], device_at(x, y + d, z, c))

    def z8_copy(n):
        ref = piece(p, 1, n)
        return remote(ref, ref, sem_z8_s.at[n], sem_z8_r.at[n], partner)

    own_tag = rowbuf.at[p, pl.ds(ROWS, 16)]
    tag_over = remote(own_tag, tags.at[y], sem_tag_s.at[0], sem_tag_r.at[0], partner)

    def tag_copy(k):
        return remote(tags.at[y], tags.at[y], sem_tag_s.at[k], sem_tag_r.at[k], device_at(x, y + k, z, c))

    def col_block(x_at, zl_at, half=None):
        at = pl.ds(pl.multiple_of((x_at * RUN + zl_at) * 16, 16), 16)
        if half is None:
            return colbuf.at[at]
        return colbuf.at[at, pl.ds(half * (KEEP // 2), KEEP // 2)]

    def inside(v):
        return jnp.logical_and(v >= 0, v < RUN)

    def c_send(way, d):
        step = 1 - 2 * way
        origin = zl - step * (0 if d == 4 else d - 1)
        jump = step * (4 if d == 4 else 1)
        ref = col_block(x, origin)
        copy = remote(
            ref, ref, sem_c_s.at[way, d - 1], sem_c_r.at[way, d - 1], device_at(x, y, z + jump, c)
        )
        go(copy, jnp.logical_and(inside(origin), inside(zl + jump)))

    def x_copy(way, x_at, zl_at, half=None):
        at = jnp.clip(zl_at, 0, RUN - 1)
        ref = col_block(x_at, zl_at, half)
        s, r = (sem_x_s, sem_x_r) if half is None else (sem_f_s, sem_f_r)
        return remote(ref, ref, s.at[way, at], r.at[way, at], device_at(x + 1 - 2 * way, y, z, c))

    def x_send(zl_at, when):
        for way in range(2):
            go(x_copy(way, x, zl_at), when)

    def x_pass(zl_at, when):
        for way in range(2):
            x_at = (x - (1 - 2 * way) + NX) % NX
            only(when, x_copy(way, x_at, zl_at).wait_recv)
            go(x_copy(way, x_at, zl_at, way), when)

    events = []

    def at_time(t, fn, *args):
        events.append((t, len(events), functools.partial(fn, *args)))

    sib_rows = remote(row_out, rowbuf.at[p, pl.ds(own_rows, ROWS)], sem_sib_s.at[0], sem_sib_r.at[0], sibling)
    sib_cols = remote(col_out, col_in, sem_sib_s.at[1], sem_sib_r.at[1], sibling)

    go(sib_rows)
    go(tag_over, upper)
    go(z8_copy(0), upper)
    go(y_copy(0, 0, 1, 0))
    go(y_copy(0, 1, 1, 0))
    loads[2].wait()
    blocks = [col_ref[k].astype(jnp.float32) for k in range(4)]
    wide = [swap_lanes(blocks[2 * q], blocks[2 * q + 1]) for q in range(2)]
    my_cols = jnp.where(c == 0, wide[0], wide[1])
    col_out[...] = jnp.where(c == 0, wide[1], wide[0]).astype(jnp.bfloat16)
    go(sib_cols)
    sib_rows.wait_recv()
    go(z8_copy(1), upper)
    go(y_copy(0, 0, 1, 1))
    go(y_copy(0, 1, 1, 1))

    def columns():
        sib_cols.wait_recv()
        other = col_in[...].astype(jnp.float32)
        both = jnp.concatenate([jnp.where(c == 0, my_cols, other), jnp.where(c == 0, other, my_cols)], axis=0)
        col_block(x, zl)[...] = both.astype(jnp.bfloat16)
        c_send(1, 1)
        c_send(1, 4)
        x_send(zl, None)

    at_time(T_SIB, columns)
    at_time(T_SIB + T_X, x_pass, zl, None)

    def y_event(stream, way, hop, n):
        y_copy(stream, way, hop, n).wait_recv()
        if hop < (4 if way == 0 else 3):
            go(y_copy(stream, way, hop + 1, n), group=late if stream else early)

    def tag_event():
        tag_over.wait_recv()
        for k in range(1, NY):
            go(tag_copy(k), group=late)
        go(tag_over, lower, late)
        go(z8_copy(0), lower, late)
        go(z8_copy(1), lower, late)

    def z8_event(n):
        z8_copy(n).wait_recv()
        go(y_copy(1, 0, 1, n), group=late)
        go(y_copy(1, 1, 1, n), group=late)

    at_time(T_P, tag_event)
    for n in range(2):
        at_time(T_P + 0.2 + n, z8_event, n)
        for stream in range(2):
            base = (0.0, T_P + 0.2)[stream] + n * (1.5, 1.0)[stream]
            for hop in range(1, 5):
                for way in range(2):
                    if hop <= (4 if way == 0 else 3):
                        at_time(base + T_Y * hop, y_event, stream, way, hop, n)

    def c_event(way, d):
        origin = zl - (1 - 2 * way) * d
        valid = inside(origin)
        ref = col_block(x, origin)
        only(valid, remote(ref, ref, sem_c_s.at[way, d - 1], sem_c_r.at[way, d - 1], sibling).wait_recv)
        if d not in (3, 7):
            c_send(way, d + 1)
        x_send(origin, valid)
        if way == 1 and d in (1, 4):
            c_send(0, d)

    def x_event(way, d):
        origin = zl - (1 - 2 * way) * d
        x_pass(origin, inside(origin))

    for d in range(1, 8):
        t = T_SIB + (T_C * d if d < 4 else T_C4 + T_C * (d - 4))
        for way, t_at in ((1, t), (0, t + (T_C if d < 4 else T_C4))):
            at_time(t_at, c_event, way, d)
            at_time(t_at + T_X, x_event, way, d)

    def halves_in():
        for way in range(2):
            for zl_at in range(RUN):
                x_copy(way, (x + 2) % NX, zl_at, way).wait_recv()

    def scores_of(tag):
        tag = tag.astype(jnp.float32)
        return tag[0:1] * 16.0 + tag[1:2]

    stats = []

    def totals():
        for k in range(1, NY):
            tag_copy(k).wait_recv()
        values = [scores_of(rowbuf[2 * i + zh, ROWS : ROWS + 16, :]) for i in range(NY)]
        values += [scores_of(tags[i]) for i in range(NY)]
        values = jnp.concatenate(values, axis=0)
        members = POP * 64
        average = jnp.sum(values) * 0.5 / members
        variance = jnp.sum(values * values) * 0.5 / members - average * average
        stats.extend((average, lax.rsqrt(variance + score_eps)))

    def weighted(slot, tag, h):
        fitness = (scores_of(tag) - stats[0]) * stats[1]
        block = rowbuf[slot, pl.ds(pl.multiple_of(h * first_len, 16), ROWS), :].astype(jnp.float32)
        return (block * fitness).astype(jnp.bfloat16)

    def times_columns(rows, first, width):
        return lax.dot_general(
            rows, colbuf[:, pl.ds(pl.multiple_of(first, 128), width)], (((1,), (1,)), ((), ())),
            preferred_element_type=jnp.float32,
        )

    def own_half():
        for i in range(NY):
            slot = 2 * i + zh
            tag = rowbuf[slot, ROWS : ROWS + 16, :]
            for h in range(2):
                wbuf[h, :, i * 128 : (i + 1) * 128] = weighted(slot, tag, h)
        for h in range(2):
            acc[h] = times_columns(wbuf[h], zh * (KEEP // 2), KEEP // 2)

    def add_block(y_at, h):
        slot = 2 * y_at + 1 - zh
        acc[h] += times_columns(weighted(slot, tags[y_at], h), (1 - zh) * (KEEP // 2) + y_at * 128, 128)

    def add_far(*hops):
        for hop in hops:
            for y_at in {0: (y,), 4: ((y - 4 * turn + NY) % NY,)}.get(
                hop, ((y - hop * turn + NY) % NY, (y + hop * turn + NY) % NY)
            ):
                for h in range(2):
                    add_block(y_at, h)

    t_last = T_P + 0.2 + 1.0
    t_cols = T_SIB + 2 * T_C4 + 3 * T_C + T_X
    at_time(t_cols, halves_in)
    at_time(t_cols, totals)
    at_time(t_cols, own_half)
    at_time(t_last + T_Y * 3 + 0.1, add_far, 0, 1, 2, 3)

    def departed(group):
        for when, copy in group:
            only(when, copy.wait_send)

    at_time(t_last + T_Y * 3 + 0.2, lambda: departed(early))

    for _, _, fn in sorted(events, key=lambda e: e[:2]):
        fn()

    last = (y - 4 * turn + NY) % NY
    add_block(last, 1 - c)
    swap = remote(acc.at[1 - c], part_in, sem_sib_s.at[2], sem_sib_r.at[2], sibling)
    swap.start()
    add_block(last, c)
    departed(late)
    swap.wait()
    out_ref[...] = (acc[c] + part_in[...]) * (1.0 / 64.0)


def local(weight, first_moment, second_moment, row_factors, column_factors, scores):
    columns = jnp.transpose(column_factors, (1, 2, 0))
    dma = pltpu.SemaphoreType.DMA
    update = pl.pallas_call(
        kernel,
        name="gather_update",
        out_shape=jax.ShapeDtypeStruct((ROWS, COLS), jnp.float32),
        in_specs=[pl.BlockSpec(memory_space=pltpu.HBM)] * 3,
        out_specs=pl.BlockSpec(memory_space=pltpu.VMEM),
        scratch_shapes=[
            pltpu.VMEM((64, 4, ROWS), jnp.bfloat16),
            pltpu.VMEM((4, 8, 1024), jnp.bfloat16),
            pltpu.VMEM((1, 64), jnp.int32),
            pltpu.VMEM((POP, SLOT, 128), jnp.bfloat16),
            pltpu.VMEM((NY, 16, 128), jnp.bfloat16),
            pltpu.VMEM((COLS, KEEP), jnp.bfloat16),
            pltpu.VMEM((ROWS, 128), jnp.bfloat16),
            pltpu.VMEM((8, KEEP), jnp.bfloat16),
            pltpu.VMEM((8, KEEP), jnp.bfloat16),
            pltpu.VMEM((2, ROWS, KEEP // 2), jnp.bfloat16),
            pltpu.VMEM((2, ROWS, COLS), jnp.float32),
            pltpu.VMEM((ROWS, COLS), jnp.float32),
            dma((3,)),
            dma((3,)), dma((3,)),
            dma((2,)), dma((2,)),
            dma((NY,)), dma((NY,)),
            dma((4, 4, 2)), dma((4, 4, 2)),
            dma((2, 7)), dma((2, 7)),
            dma((2, RUN)), dma((2, RUN)),
            dma((2, RUN)), dma((2, RUN)),
        ],
        compiler_params=pltpu.CompilerParams(
            collective_id=0, has_side_effects=True, vmem_limit_bytes=60 * 2**20
        ),
        cost_estimate=pl.CostEstimate(flops=2 * ROWS * COLS * 4096, bytes_accessed=2**20, transcendentals=0),
    )(row_factors, columns, scores.reshape(1, 64))
    new_first = beta_one * first_moment + (1.0 - beta_one) * update
    new_second = beta_two * second_moment + (1.0 - beta_two) * update * update
    corrected_first = new_first / (1.0 - beta_one**ADAM_STEP)
    corrected_second = new_second / (1.0 - beta_two**ADAM_STEP)
    new_weight = weight + learn_rate * corrected_first / (jnp.sqrt(corrected_second) + adam_eps)
    return (new_weight, new_first, new_second)


def solution(mesh):
    in_specs = (
        P("fsdp", "pop"),
        P("fsdp", "pop"),
        P("fsdp", "pop"),
        P("pop", None, "fsdp"),
        P(None, None, ("pop", "fsdp")),
        P("pop"),
    )
    out_specs = (P("fsdp", "pop"), P("fsdp", "pop"), P("fsdp", "pop"))
    return jax.shard_map(local, mesh=mesh, in_specs=in_specs, out_specs=out_specs, check_vma=False)
```

time: 374 us -> 66.3 us (0.18)
  waiting for transfers between devices: 267 us -> 0 us
  blocking collectives: 80.5 us -> 0 us
  Pallas kernels: 0 us -> 63.1 us
  between operations: 16.7 us -> 0.69 us
  matrix products: 5.91 us -> 0 us
    all_gather x2 -> x0, waiting for transfers between devices: 266 us -> none  [the longest x1 145 us: local(): left_rows = lax.all_gather(local_weighted, 'pop', axis=0, tiled=True)]
    psum x1 -> x0, blocking collectives: 80.5 us -> none  [local(): lax.psum((jnp.sum(values), jnp.sum(values * values)), 'pop')]
    pallas_call x0 -> x1, Pallas kernels: none -> 63.1 us  [local(): pl.pallas_call(kernel, name='gather_update', out_shape=jax.ShapeDtypeStru...]
    dot_general x1 -> x0, matrix products: 5.91 us -> none  [local(): lax.dot_general(left_rows.reshape(count * factor_rank, row_count), column...]
  transfers between devices with their start and end apart: 2 -> 0, of which waited for: 2 -> 0; matrix products, arithmetic and copies ran while one was open for 0% -> 0% of each run, Pallas kernels for 0% -> 0%
where the time goes in v2:
time: 66.3 us; the launch traced here: 66.1 us
  Pallas kernels  63.1 us (95%)
  other arithmetic  2.29 us (3%)
  between operations  0.69 us (1%)
    pallas_call x1, Pallas kernels, local(): pl.pallas_call(kernel, name='gather_update', out_shape=jax.ShapeDtypeStru...  63.1 us
    add x1, other arithmetic, local(): weight + learn_rate * corrected_first / (jnp.sqrt(corrected_second) + ada...  2.29 us

profile of v2, /device:TPU:1, one launch (start us, length us, event | category | flops | bytes accessed | tf_op | source)
XLA Modules:
  0.0 66.1 jit_solution(1052633537766894711)
XLA Ops:
  0.6 0.0 copy-start
  0.6 0.0 copy-start.1
  0.7 0.0 copy-start.2
  0.7 63.1 %gather_update.1 = f32[224,512]{1,0:T(8,128)} custom-call(bf16[64,4,224]{2,1,0:T(4,128)(2,1)} %row_hbm.1, bf16[4,8,1024]{2,1,0:T(8,128)(2,1)} %bitcast.2, s32[1,64]{1,0:T(1,128)} %bitcast.3), custom_call_target="tpu_custom_call" | custom-call | flops 939524096 | bytes 1048576 | tf_op jit(solution)/shard_map/gather_update/pallas_call | solution.py:343
  63.8 0.0 copy-done
  63.8 0.0 copy-done.1
  63.8 0.0 copy-done.2
  63.8 2.3 %divide_add_fusion = (f32[224,512]{1,0:T(8,128)}, f32[224,512]{1,0:T(8,128)}, f32[224,512]{1,0:T(8,128)}) fusion(f32[224,512]{1,0:T(8,128)S(1)} %copy-done, f32[224,512]{1,0:T(8,128)} %gather_update.1, f32[224,512]{1,0:T(8,128)S(1)} %copy-done.1, f32[224,512]{1,0:T(8,128)S(1)} %copy-done.2), kind=kLoop, calls=%fused_computation.2 | loop fusion | flops 1376256 | bytes 3211264 | tf_op jit(solution)/shard_map/add | solution.py:380
Async XLA Ops:
  0.6 63.2 %copy-start = (f32[224,512]{1,0:T(8,128)S(1)}, f32[224,512]{1,0:T(8,128)}, u32[]{:S(2)}) copy-start(f32[224,512]{1,0:T(8,128)} %param.6) | copy-start | bytes 1376260
  0.6 63.2 %copy-start.1 = (f32[224,512]{1,0:T(8,128)S(1)}, f32[224,512]{1,0:T(8,128)}, u32[]{:S(2)}) copy-start(f32[224,512]{1,0:T(8,128)} %param.7) | copy-start | bytes 1376260
  0.7 63.2 %copy-start.2 = (f32[224,512]{1,0:T(8,128)S(1)}, f32[224,512]{1,0:T(8,128)}, u32[]{:S(2)}) copy-start(f32[224,512]{1,0:T(8,128)} %param.8) | copy-start | bytes 1376260

commit v3 on v0

v3 whole, which is shorter than its diff:
```python
import functools
import math

import jax
import jax.numpy as jnp
from jax import lax
from jax.experimental import pallas as pl
from jax.experimental.pallas import tpu as pltpu
from jax.sharding import PartitionSpec as P

ADAM_STEP = 10
MESH = pl.DeviceIdType.MESH

beta_one = 0.9
beta_two = 0.999
learn_rate = 0.05
adam_eps = 1e-08
score_eps = 1e-05

NX, NY, NZ, RUN = 4, 8, 16, 8
POP = 16
ROWS = 224
COLS = 512
DEPTH = 4096
TAG = 16
SLOT = TAG + 2 * ROWS
T_Y, T_C, T_HOP, T_X, T_COL, T_P = 2.9, 3.0, 0.5, 3.0, 2.0, 15.0
DIRECT, HALF, SPLIT = 5, 0.7, 0
PARENT = ({1: 0, 4: 0, 2: 1, 3: 2, 5: 4, 6: 5, 7: 6},) * 2


def device_at(x, y, z, c):
    x, y, z = (x + NX) % NX, (y + NY) % NY, (z + NZ) % NZ
    return (y * 2 + z // RUN, (x * RUN + z % RUN) * 2 + c)


def ordered(ranks):
    low = lax.broadcasted_iota(jnp.int32, (8, 128), 1) < 64
    parts = [[], []]
    for t in range(8):
        for q in range(2):
            a = ranks[2 * q][:, t * 128 : (t + 1) * 128]
            b = ranks[2 * q + 1][:, t * 128 : (t + 1) * 128]
            parts[0].append(jnp.where(low, a, pltpu.roll(b, 64, 1)))
            parts[1].append(jnp.where(low, pltpu.roll(a, 64, 1), b))
    return jnp.concatenate(parts[0] + parts[1], axis=1)


def kernel(
    row_hbm, col_hbm, score_hbm, out_ref,
    row_ref, col_ref, score_ref, rowbuf, tags, colbuf, col_out, col_in, wbuf, acc,
    sem_in, sem_sib_s, sem_sib_r, sem_z8_s, sem_z8_r, sem_tag_s, sem_tag_r, sem_y_s, sem_y_r,
    sem_push_s, sem_push_r, sem_pc_s, sem_pc_r, sem_c_s, sem_c_r, sem_x_s, sem_x_r, sem_f_s, sem_f_r, sem_ack,
):
    p = lax.axis_index("pop")
    f = lax.axis_index("fsdp")
    y, zh = p // 2, p % 2
    c, zl, x = f % 2, (f // 2) % RUN, f // (2 * RUN)
    z = zh * RUN + zl
    upper, lower = zh == 1, zh == 0
    column_core, row_core = c == 0, c == 1

    loads = [
        pltpu.make_async_copy(src, dst, sem_in.at[i])
        for i, (src, dst) in enumerate(((row_hbm, row_ref), (score_hbm, score_ref), (col_hbm, col_ref)))
    ]
    for load in loads:
        load.start()

    sibling = device_at(x, y, z, 1 - c)
    far_rows = device_at(x, y, z + 8, 1)
    barrier = pltpu.get_barrier_semaphore()

    def greet(*dev):
        pl.semaphore_signal(barrier, inc=1, device_id=device_at(*dev), device_id_type=MESH)

    greet(x, y, z, 1 - c)

    @pl.when(column_core)
    def _():
        greet(x + 1, y, z, 0)
        greet(x - 1, y, z, 0)
        pl.when(zl < 7)(lambda: greet(x, y, z + 1, 0))
        pl.when(zl < 4)(lambda: greet(x, y, z + 4, 0))
        if PARENT[1][2] == 0:
            pl.when(zl < 6)(lambda: greet(x, y, z + 2, 0))

    @pl.when(row_core)
    def _():
        greet(x, y + 1, z, 1)
        greet(x, y - 1, z, 1)

        @pl.when(lower)
        def _():
            greet(x, y, z + 8, 0)
            greet(x, y, z + 8, 1)

    below = jnp.where(zl > 0, 1, 0) + jnp.where(zl >= 4, 1, 0)
    if PARENT[1][2] == 0:
        below = below + jnp.where(zl >= 2, 1, 0)
    expected = 3 + zh + jnp.where(column_core, below, 0)

    loads[0].wait()
    loads[1].wait()
    rows = row_ref[...].astype(jnp.float32)
    own_rows = pl.multiple_of(TAG + c * ROWS, 16)
    for q in range(2):
        rowbuf[q, p, pl.ds(own_rows, ROWS), :] = jnp.concatenate([rows[:, 2 * q, :], rows[:, 2 * q + 1, :]], axis=0).T.astype(jnp.bfloat16)
    score = score_ref[...]
    score = jnp.concatenate([score, score], axis=1)
    line = lax.broadcasted_iota(jnp.int32, (TAG, 128), 0)
    coded = jnp.where(line == 0, score // 16, jnp.where(line == 1, score % 16, 0))
    rowbuf[0, p, 0:TAG, :] = coded.astype(jnp.float32).astype(jnp.bfloat16)

    pl.semaphore_wait(barrier, expected)

    def remote(src, dst, s_sem, r_sem, dev):
        return pltpu.make_async_remote_copy(
            src_ref=src, dst_ref=dst, send_sem=s_sem, recv_sem=r_sem, device_id=dev, device_id_type=MESH
        )

    def only(when, fn):
        if when is None:
            fn()
        else:
            pl.when(when)(fn)

    def inside(v):
        return jnp.logical_and(v >= 0, v < RUN)

    def z8_copy(q, n):
        ref = rowbuf.at[q, p, pl.ds(TAG + n * ROWS, ROWS)]
        return remote(ref, ref, sem_z8_s.at[q, n], sem_z8_r.at[q, n], far_rows)

    sib_rows = remote(
        rowbuf.at[:, p, pl.ds(TAG, ROWS)], rowbuf.at[:, p, pl.ds(TAG, ROWS)], sem_sib_s.at[0], sem_sib_r.at[0], sibling
    )
    sib_cols = remote(col_out, col_in, sem_sib_s.at[1], sem_sib_r.at[1], sibling)

    def own_columns():
        loads[2].wait()
        return ordered([col_ref[k].astype(jnp.float32) for k in range(4)])

    def scores_of(tag):
        tag = tag.astype(jnp.float32)
        return tag[0:1] * 16.0 + tag[1:2]

    def totals():
        values = [scores_of(rowbuf[0, 2 * i + zh, 0:TAG, :]) for i in range(NY)]
        values += [scores_of(tags[i]) for i in range(NY)]
        values = jnp.concatenate(values, axis=0)
        members = POP * 64
        average = jnp.sum(values) * 0.5 / members
        variance = jnp.sum(values * values) * 0.5 / members - average * average
        return average, lax.rsqrt(variance + score_eps)

    def weighted(slot, tag, stats):
        fitness = (scores_of(tag) - stats[0]) * stats[1]
        blocks = [rowbuf[q, slot, pl.ds(own_rows, ROWS), :].astype(jnp.float32) * fitness for q in range(2)]
        return jnp.concatenate(blocks, axis=1).astype(jnp.bfloat16)

    def times_columns(first, width):
        at = pl.ds(pl.multiple_of(first, 128), width)
        return lax.dot_general(
            wbuf[:, at], colbuf[:, at], (((1,), (1,)), ((), ())), preferred_element_type=jnp.float32
        )

    def weigh_own(stats):
        for i in range(NY):
            slot = 2 * i + zh
            wbuf[:, pl.ds(pl.multiple_of(zh * (DEPTH // 2) + i * 256, 256), 256)] = weighted(
                slot, rowbuf[0, slot, 0:TAG, :], stats
            )

    def weigh(y_at, stats):
        at = pl.ds(pl.multiple_of((1 - zh) * (DEPTH // 2) + y_at * 256, 256), 256)
        wbuf[:, at] = weighted(2 * y_at + 1 - zh, tags[y_at], stats)

    def hops_of(q, way):
        return 4 if q == way else 3

    def source_y(way, hop):
        return (y - (1 - 2 * way) * hop + NY) % NY

    def slot_of(stream, y_at):
        return y_at * 2 + (zh if stream == 0 else 1 - zh)

    def push(stream, q, y_at, sem):
        at = pl.ds(0, TAG + ROWS) if stream == 0 and q == 0 else pl.ds(TAG, ROWS)
        ref = rowbuf.at[q, slot_of(stream, y_at), at]
        return remote(ref, ref, sem_push_s.at[sem], sem_push_r.at[sem], sibling)

    tag_push = remote(tags, tags, sem_push_s.at[4], sem_push_r.at[4], sibling)

    class Schedule:
        def __init__(self):
            self.sent, self.events = [], []

        def go(self, copy, when=None):
            only(when, copy.start)
            self.sent.append((when, copy))

        def at(self, t, fn, *args):
            self.events.append((t, len(self.events), functools.partial(fn, *args)))

        def run(self):
            for _, _, fn in sorted(self.events, key=lambda e: e[:2]):
                fn()

        def departed(self):
            for when, copy in self.sent:
                only(when, copy.wait_send)
            self.sent = []

    def weigh_near(stats):
        for hop in range(4):
            for way in range(2 if hop else 1):
                weigh(source_y(way, hop), stats)

    @pl.when(row_core)
    def _():
        s = Schedule()
        own_tag = rowbuf.at[0, p, pl.ds(0, TAG)]
        tag_over = remote(own_tag, tags.at[y], sem_tag_s.at[0], sem_tag_r.at[0], far_rows)

        def tag_copy(k):
            return remote(tags.at[y], tags.at[y], sem_tag_s.at[k], sem_tag_r.at[k], device_at(x, y + k, z, 1))

        def y_copy(stream, q, way, hop, n=None):
            if n is None:
                at = pl.ds(0, SLOT) if stream == 0 and q == 0 else pl.ds(TAG, 2 * ROWS)
            else:
                at = pl.ds(TAG + n * ROWS, ROWS)
            ref = rowbuf.at[q, slot_of(stream, source_y(way, hop - 1)), at]
            i = stream * 2 + q + (2 if n == 1 else 0)
            return remote(
                ref, ref, sem_y_s.at[i, way, hop - 1], sem_y_r.at[i, way, hop - 1], device_at(x, y + 1 - 2 * way, z, 1)
            )

        s.go(tag_over, upper)
        s.go(z8_copy(0, 1), upper)
        s.go(z8_copy(1, 1), upper)
        col_out[...] = own_columns().astype(jnp.bfloat16)
        s.go(sib_cols)
        sib_rows.wait_recv()
        for q in range(2):
            for way in range(2):
                s.go(y_copy(0, q, way, 1))

        def y_event(stream, q, way, hop, n=None):
            y_copy(stream, q, way, hop, n).wait_recv()
            if hop < hops_of(q, way):
                s.go(y_copy(stream, q, way, hop + 1, n))
            if n == 1:
                return
            if stream == 0:
                sem = 0
            else:
                sem = 1 if hop < 4 else 2 + q
            s.go(push(stream, q, source_y(way, hop), sem))

        def tag_event():
            tag_over.wait_recv()
            for k in range(1, NY):
                s.go(tag_copy(k))
            s.go(tag_over, lower)
            for q in range(2):
                for n in range(2):
                    s.go(z8_copy(q, n), lower)

        def z8_event(q):
            if not SPLIT:
                for n in range(2):
                    z8_copy(q, n).wait_recv()
                for way in range(2):
                    s.go(y_copy(1, q, way, 1))
            else:
                for n in (1, 0):
                    z8_copy(q, n).wait_recv()
                    for way in range(2):
                        s.go(y_copy(1, q, way, 1, n))
            s.go(push(1, q, y, 1))

        def tags_in():
            for k in range(1, NY):
                tag_copy(k).wait_recv()
            s.go(tag_push)

        s.at(T_P, tag_event)
        s.at(T_P + 5.0, tags_in)
        for q in range(2):
            s.at(T_P + 0.5 + q * 0.5, z8_event, q)
            for stream in range(2):
                base = (2.0, T_P + 0.5)[stream] + 0.5 * q
                for hop in range(1, 5):
                    for way in range(2):
                        if hop <= hops_of(q, way):
                            for n in (1, 0) if stream and SPLIT else (None,):
                                s.at(base + T_Y * hop, y_event, stream, q, way, hop, n)
        s.run()
        stats = totals()
        weigh_own(stats)
        weigh_near(stats)
        weigh(source_y(0, 4), stats)
        remote(colbuf, colbuf, sem_pc_s, sem_pc_r, sibling).wait_recv()
        out_ref[...] = times_columns(0, DEPTH) * (1.0 / 64.0)
        s.departed()

    @pl.when(column_core)
    def _():
        s = Schedule()

        def col_block(x_at, zl_at, half=None):
            at = pl.ds(pl.multiple_of((x_at * RUN + zl_at) * 16, 16), 16)
            if half is None:
                return colbuf.at[at]
            return colbuf.at[at, pl.ds(half * (DEPTH // 2), DEPTH // 2)]

        def push_block(x_at, zl_at, when, half=None):
            ref = col_block(x_at, zl_at, half)
            s.go(remote(ref, ref, sem_pc_s, sem_pc_r, sibling), when)

        def c_send(way, d, half):
            step = 1 - 2 * way
            origin = zl - step * PARENT[way][d]
            jump = step * (d - PARENT[way][d])
            ref = col_block(x, origin, half)
            copy = remote(
                ref, ref, sem_c_s.at[way, d - 1, half], sem_c_r.at[way, d - 1, half], device_at(x, y, z + jump, 0)
            )
            s.go(copy, jnp.logical_and(inside(origin), inside(zl + jump)))

        def x_copy(way, x_at, zl_at, half):
            at = jnp.clip(zl_at, 0, RUN - 1)
            ref = col_block(x_at, zl_at, half)
            return remote(
                ref, ref, sem_x_s.at[way, at, half], sem_x_r.at[way, at, half], device_at(x + 1 - 2 * way, y, z, 0)
            )

        def far_copy(zl_at, half, x_at, straight):
            at = jnp.clip(zl_at, 0, RUN - 1)
            ref = col_block(x_at, zl_at, half)
            to = device_at(x + (2 if straight else 1 - 2 * half), y, z, 0)
            return remote(ref, ref, sem_f_s.at[at, half], sem_f_r.at[at, half], to)

        def x_send(zl_at, when, half, straight):
            for way in range(2):
                s.go(x_copy(way, x, zl_at, half), when)
            if straight:
                s.go(far_copy(zl_at, half, x, True), when)

        def x_pass(zl_at, when, half, straight):
            for way in (half, 1 - half):
                x_at = (x - (1 - 2 * way) + NX) % NX
                only(when, x_copy(way, x_at, zl_at, half).wait_recv)
                if way == half and not straight:
                    s.go(far_copy(zl_at, half, x_at, False), when)
                push_block(x_at, zl_at, when, half)

        pl.when(zl > 0)(
            lambda: pl.semaphore_signal(sem_ack.at[0], inc=1, device_id=device_at(x, y, z - 1, 0), device_id_type=MESH)
        )
        pl.when(zl >= 4)(
            lambda: pl.semaphore_signal(sem_ack.at[1], inc=1, device_id=device_at(x, y, z - 4, 0), device_id_type=MESH)
        )
        for q in range(2):
            s.go(z8_copy(q, 0), upper)
        s.go(sib_rows)
        mine = own_columns()
        sib_cols.wait_recv()
        both = jnp.concatenate([mine, col_in[...].astype(jnp.float32)], axis=0)
        col_block(x, zl)[...] = both.astype(jnp.bfloat16)
        for half in range(2):
            c_send(1, 1, half)
            x_send(zl, None, half, DIRECT <= 0)
        for d in (4, 2):
            if PARENT[1][d] == 0:
                c_send(1, d, 0)
                c_send(1, d, 1)
        for half in range(2):
            push_block(x, zl, None, half)

        def up_near():
            pl.when(zl < 7)(lambda: pl.semaphore_wait(sem_ack.at[0], 1))
            for half in range(2):
                c_send(0, 1, half)

        def up_far():
            pl.when(zl < 4)(lambda: pl.semaphore_wait(sem_ack.at[1], 1))
            for half in range(2):
                c_send(0, 4, half)

        def c_event(way, d, half):
            origin = zl - (1 - 2 * way) * d
            valid = inside(origin)
            ref = col_block(x, origin, half)
            only(valid, remote(ref, ref, sem_c_s.at[way, d - 1, half], sem_c_r.at[way, d - 1, half], sibling).wait_recv)
            for e in range(d + 1, RUN):
                if PARENT[way][e] == d:
                    c_send(way, e, half)
            x_send(origin, valid, half, d >= DIRECT)
            push_block(x, origin, valid, half)

        def x_event(way, d, half):
            origin = zl - (1 - 2 * way) * d
            x_pass(origin, inside(origin), half, d >= DIRECT)

        s.at(T_COL + 0.1, up_near)
        s.at(T_COL + 1.5, up_far)
        for half in range(2):
            s.at(T_COL + T_X + HALF * half, x_pass, zl, None, half, DIRECT <= 0)
            for way in range(2):
                arrives = {0: T_COL + HALF * half + 0.7 * (1 - way)}
                for d in range(1, RUN):
                    before = PARENT[way][d]
                    arrives[d] = arrives[before] + T_C + T_HOP * (d - before - 1)
                    s.at(arrives[d], c_event, way, d, half)
                    s.at(arrives[d] + T_X, x_event, way, d, half)
        s.run()
        for zl_at in range(RUN):
            for way in range(2):
                far_copy(zl_at, way, (x + 2) % NX, True).wait_recv()
                push_block((x + 2) % NX, zl_at, None, way)
        remote(
            rowbuf.at[0, pl.ds(0, 7)], rowbuf.at[0, pl.ds(0, 7)], sem_push_s.at[0], sem_push_r.at[0], sibling
        ).wait_recv()
        tag_push.wait_recv()
        stats = totals()
        weigh_own(stats)
        acc[...] = times_columns(zh * (DEPTH // 2), DEPTH // 2)
        most = rowbuf.at[:, pl.ds(0, 7), pl.ds(TAG, ROWS)]
        remote(most, most, sem_push_s.at[1], sem_push_r.at[1], sibling).wait_recv()
        weigh_near(stats)
        for q in range(2):
            push(1, q, source_y(q, 4), 2 + q).wait_recv()
        weigh(source_y(0, 4), stats)
        out_ref[...] = (acc[...] + times_columns((1 - zh) * (DEPTH // 2), DEPTH // 2)) * (1.0 / 64.0)
        s.departed()


def local(weight, first_moment, second_moment, row_factors, column_factors, scores):
    columns = jnp.transpose(column_factors, (1, 2, 0))
    dma = pltpu.SemaphoreType.DMA
    update = pl.pallas_call(
        kernel,
        name="gather_update",
        out_shape=jax.ShapeDtypeStruct((ROWS, COLS), jnp.float32),
        in_specs=[pl.BlockSpec(memory_space=pltpu.HBM)] * 3,
        out_specs=pl.BlockSpec(memory_space=pltpu.VMEM),
        scratch_shapes=[
            pltpu.VMEM((64, 4, ROWS), jnp.bfloat16),
            pltpu.VMEM((4, 8, 1024), jnp.bfloat16),
            pltpu.VMEM((1, 64), jnp.int32),
            pltpu.VMEM((2, POP, SLOT, 128), jnp.bfloat16),
            pltpu.VMEM((NY, TAG, 128), jnp.bfloat16),
            pltpu.VMEM((COLS, DEPTH), jnp.bfloat16),
            pltpu.VMEM((8, DEPTH), jnp.bfloat16),
            pltpu.VMEM((8, DEPTH), jnp.bfloat16),
            pltpu.VMEM((ROWS, DEPTH), jnp.bfloat16),
            pltpu.VMEM((ROWS, COLS), jnp.float32),
            dma((3,)),
            dma((2,)), dma((2,)),
            dma((2, 2)), dma((2, 2)),
            dma((NY,)), dma((NY,)),
            dma((6, 2, 4)), dma((6, 2, 4)),
            dma((5,)), dma((5,)),
            dma, dma,
            dma((2, 7, 2)), dma((2, 7, 2)),
            dma((2, RUN, 2)), dma((2, RUN, 2)),
            dma((RUN, 2)), dma((RUN, 2)),
            pltpu.SemaphoreType.REGULAR((2,)),
        ],
        compiler_params=pltpu.CompilerParams(
            collective_id=0, has_side_effects=True, vmem_limit_bytes=60 * 2**20
        ),
        cost_estimate=pl.CostEstimate(flops=2 * ROWS * COLS * 4096, bytes_accessed=2**20, transcendentals=0),
    )(row_factors, columns, scores.reshape(1, 64))
    new_first = beta_one * first_moment + (1.0 - beta_one) * update
    new_second = beta_two * second_moment + (1.0 - beta_two) * update * update
    corrected_first = new_first / (1.0 - beta_one**ADAM_STEP)
    corrected_second = new_second / (1.0 - beta_two**ADAM_STEP)
    new_weight = weight + learn_rate * corrected_first / (jnp.sqrt(corrected_second) + adam_eps)
    return (new_weight, new_first, new_second)


def solution(mesh):
    in_specs = (
        P("fsdp", "pop"),
        P("fsdp", "pop"),
        P("fsdp", "pop"),
        P("pop", None, "fsdp"),
        P(None, None, ("pop", "fsdp")),
        P("pop"),
    )
    out_specs = (P("fsdp", "pop"), P("fsdp", "pop"), P("fsdp", "pop"))
    return jax.shard_map(local, mesh=mesh, in_specs=in_specs, out_specs=out_specs, check_vma=False)
```

time: 374 us -> 60.1 us (0.16)
  waiting for transfers between devices: 267 us -> 0 us
  blocking collectives: 80.5 us -> 0 us
  Pallas kernels: 0 us -> 56.9 us
  between operations: 16.7 us -> 0.69 us
  matrix products: 5.91 us -> 0 us
    all_gather x2 -> x0, waiting for transfers between devices: 266 us -> none  [the longest x1 145 us: local(): left_rows = lax.all_gather(local_weighted, 'pop', axis=0, tiled=True)]
    psum x1 -> x0, blocking collectives: 80.5 us -> none  [local(): lax.psum((jnp.sum(values), jnp.sum(values * values)), 'pop')]
    pallas_call x0 -> x1, Pallas kernels: none -> 56.9 us  [local(): pl.pallas_call(kernel, name='gather_update', out_shape=jax.ShapeDtypeStru...]
    dot_general x1 -> x0, matrix products: 5.91 us -> none  [local(): lax.dot_general(left_rows.reshape(count * factor_rank, row_count), column...]
  transfers between devices with their start and end apart: 2 -> 0, of which waited for: 2 -> 0; matrix products, arithmetic and copies ran while one was open for 0% -> 0% of each run, Pallas kernels for 0% -> 0%
where the time goes in v3:
time: 60.1 us; the launch traced here: 59.9 us
  Pallas kernels  56.9 us (95%)
  other arithmetic  2.29 us (4%)
  between operations  0.69 us (1%)
    pallas_call x1, Pallas kernels, local(): pl.pallas_call(kernel, name='gather_update', out_shape=jax.ShapeDtypeStru...  56.9 us
    add x1, other arithmetic, local(): weight + learn_rate * corrected_first / (jnp.sqrt(corrected_second) + ada...  2.29 us

profile of v3, /device:TPU:1, one launch (start us, length us, event | category | flops | bytes accessed | tf_op | source)
XLA Modules:
  0.0 59.9 jit_solution(6226729791698783002)
XLA Ops:
  0.6 0.0 copy-start
  0.6 0.0 copy-start.1
  0.7 0.0 copy-start.2
  0.7 56.9 %gather_update.1 = f32[224,512]{1,0:T(8,128)} custom-call(bf16[64,4,224]{2,1,0:T(4,128)(2,1)} %row_hbm.1, bf16[4,8,1024]{2,1,0:T(8,128)(2,1)} %bitcast.2, s32[1,64]{1,0:T(1,128)} %bitcast.3), custom_call_target="tpu_custom_call" | custom-call | flops 939524096 | bytes 1048576 | tf_op jit(solution)/shard_map/gather_update/pallas_call | solution.py:444
  57.6 0.0 copy-done
  57.6 0.0 copy-done.1
  57.6 0.0 copy-done.2
  57.6 2.3 %divide_add_fusion = (f32[224,512]{1,0:T(8,128)}, f32[224,512]{1,0:T(8,128)}, f32[224,512]{1,0:T(8,128)}) fusion(f32[224,512]{1,0:T(8,128)S(1)} %copy-done, f32[224,512]{1,0:T(8,128)} %gather_update.1, f32[224,512]{1,0:T(8,128)S(1)} %copy-done.1, f32[224,512]{1,0:T(8,128)S(1)} %copy-done.2), kind=kLoop, calls=%fused_computation.2 | loop fusion | flops 1376256 | bytes 3211264 | tf_op jit(solution)/shard_map/add | solution.py:482
Async XLA Ops:
  0.6 56.9 %copy-start = (f32[224,512]{1,0:T(8,128)S(1)}, f32[224,512]{1,0:T(8,128)}, u32[]{:S(2)}) copy-start(f32[224,512]{1,0:T(8,128)} %param.6) | copy-start | bytes 1376260
  0.6 56.9 %copy-start.1 = (f32[224,512]{1,0:T(8,128)S(1)}, f32[224,512]{1,0:T(8,128)}, u32[]{:S(2)}) copy-start(f32[224,512]{1,0:T(8,128)} %param.7) | copy-start | bytes 1376260
  0.7 56.9 %copy-start.2 = (f32[224,512]{1,0:T(8,128)S(1)}, f32[224,512]{1,0:T(8,128)}, u32[]{:S(2)}) copy-start(f32[224,512]{1,0:T(8,128)} %param.8) | copy-start | bytes 1376260

commit v4 on v3

--- a/solution.py
+++ b/solution.py
@@ -25,6 +25,7 @@
 TAG = 16
 SLOT = TAG + 2 * ROWS
 T_Y, T_C, T_HOP, T_X, T_COL, T_P = 2.9, 3.0, 0.5, 3.0, 2.0, 15.0
+T_FAR = 4.0
 DIRECT, HALF, SPLIT = 5, 0.7, 0
 PARENT = ({1: 0, 4: 0, 2: 1, 3: 2, 5: 4, 6: 5, 7: 6},) * 2
 
@@ -405,10 +406,19 @@
             origin = zl - (1 - 2 * way) * d
             x_pass(origin, inside(origin), half, d >= DIRECT)
 
+        def far_in(zl_at, when, half):
+            only(when, far_copy(zl_at, half, (x + 2) % NX, True).wait_recv)
+            push_block((x + 2) % NX, zl_at, when, half)
+
+        def far_event(way, d, half):
+            origin = zl - (1 - 2 * way) * d
+            far_in(origin, inside(origin), half)
+
         s.at(T_COL + 0.1, up_near)
         s.at(T_COL + 1.5, up_far)
         for half in range(2):
             s.at(T_COL + T_X + HALF * half, x_pass, zl, None, half, DIRECT <= 0)
+            s.at(T_COL + T_X + HALF * half + T_FAR, far_in, zl, None, half)
             for way in range(2):
                 arrives = {0: T_COL + HALF * half + 0.7 * (1 - way)}
                 for d in range(1, RUN):
@@ -416,11 +426,8 @@
                     arrives[d] = arrives[before] + T_C + T_HOP * (d - before - 1)
                     s.at(arrives[d], c_event, way, d, half)
                     s.at(arrives[d] + T_X, x_event, way, d, half)
+                    s.at(arrives[d] + T_X + T_FAR, far_event, way, d, half)
         s.run()
-        for zl_at in range(RUN):
-            for way in range(2):
-                far_copy(zl_at, way, (x + 2) % NX, True).wait_recv()
-                push_block((x + 2) % NX, zl_at, None, way)
         remote(
             rowbuf.at[0, pl.ds(0, 7)], rowbuf.at[0, pl.ds(0, 7)], sem_push_s.at[0], sem_push_r.at[0], sibling
         ).wait_recv()

time: 60.1 us -> 59.7 us (level)
  no operation moved by 1% of the time
where the time goes in v4:
time: 59.7 us; the launch traced here: 59.5 us
  Pallas kernels  56.5 us (95%)
  other arithmetic  2.29 us (4%)
  between operations  0.69 us (1%)
    pallas_call x1, Pallas kernels, local(): pl.pallas_call(kernel, name='gather_update', out_shape=jax.ShapeDtypeStru...  56.5 us
    add x1, other arithmetic, local(): weight + learn_rate * corrected_first / (jnp.sqrt(corrected_second) + ada...  2.29 us

profile of v4, /device:TPU:1, one launch (start us, length us, event | category | flops | bytes accessed | tf_op | source)
XLA Modules:
  0.0 59.5 jit_solution(11827735141868834694)
XLA Ops:
  0.6 0.0 copy-start
  0.6 0.0 copy-start.1
  0.7 0.0 copy-start.2
  0.7 56.5 %gather_update.1 = f32[224,512]{1,0:T(8,128)} custom-call(bf16[64,4,224]{2,1,0:T(4,128)(2,1)} %row_hbm.1, bf16[4,8,1024]{2,1,0:T(8,128)(2,1)} %bitcast.2, s32[1,64]{1,0:T(1,128)} %bitcast.3), custom_call_target="tpu_custom_call" | custom-call | flops 939524096 | bytes 1048576 | tf_op jit(solution)/shard_map/gather_update/pallas_call | solution.py:451
  57.2 0.0 copy-done
  57.2 0.0 copy-done.1
  57.2 0.0 copy-done.2
  57.2 2.3 %divide_add_fusion = (f32[224,512]{1,0:T(8,128)}, f32[224,512]{1,0:T(8,128)}, f32[224,512]{1,0:T(8,128)}) fusion(f32[224,512]{1,0:T(8,128)S(1)} %copy-done, f32[224,512]{1,0:T(8,128)} %gather_update.1, f32[224,512]{1,0:T(8,128)S(1)} %copy-done.1, f32[224,512]{1,0:T(8,128)S(1)} %copy-done.2), kind=kLoop, calls=%fused_computation.2 | loop fusion | flops 1376256 | bytes 3211264 | tf_op jit(solution)/shard_map/add | solution.py:489
Async XLA Ops:
  0.6 56.6 %copy-start = (f32[224,512]{1,0:T(8,128)S(1)}, f32[224,512]{1,0:T(8,128)}, u32[]{:S(2)}) copy-start(f32[224,512]{1,0:T(8,128)} %param.6) | copy-start | bytes 1376260
  0.6 56.6 %copy-start.1 = (f32[224,512]{1,0:T(8,128)S(1)}, f32[224,512]{1,0:T(8,128)}, u32[]{:S(2)}) copy-start(f32[224,512]{1,0:T(8,128)} %param.7) | copy-start | bytes 1376260
  0.7 56.6 %copy-start.2 = (f32[224,512]{1,0:T(8,128)S(1)}, f32[224,512]{1,0:T(8,128)}, u32[]{:S(2)}) copy-start(f32[224,512]{1,0:T(8,128)} %param.8) | copy-start | bytes 1376260
